TPU v7x, 32 devices: a whole 2x2x4 slice. The times are simulated.
32 devices in a mesh: gx: 8 (over z, x), gz: 4 (over y, core).
Axes of the slice: x: 2, y: 2, z: 4, core: 2. Of those that a mesh axis runs over, the one named last changes fastest.
Arguments:
- state: float32 [5, 32, 32, 2048], P(None, 'gx', None, 'gz'), as said below
- mask_x: int32 [32, 32, 2048], P('gx', None, 'gz'), may hold values from 0 to 1, as said below
- mask_y: int32 [32, 32, 2048], P('gx', None, 'gz'), may hold values from 0 to 1, as said below
- span_filter: float32 [1024], replicated, may hold values from 0.25 to 1
Outputs:
- updated: float32 [5, 32, 32, 2048], P(None, 'gx', None, 'gz')
Inputs may be any that keep to these rules, and one draw needn't show every extreme that they name: `state`: density and pressure of every cell lie between 0.5 and 2; the streamwise velocity lies between 0.8 and 3.2, the others between -1.2 and 1.2. `mask_x`: 1 selects the upwind value at that face, 0 the central one. `mask_y`: 1 selects the upwind value at that face, 0 the central one.
All inputs are finite; a program needn't handle non-finite values.
Results may differ from a plain program's by a relative error of at most 0.0003.
Values sent between devices are 32-bit elements; how exact they have to be, the bound alone decides.
No kernel may reach another device: no remote copies, remote signals or barrier semaphores. Data moves between devices by JAX's collectives and lax.ppermute only.
A program may use at most 64 MiB of HBM per device.

v0:
```python
import functools

import jax
import jax.numpy as jnp
import numpy as np
from jax import lax
from jax.experimental import pallas as pl
from jax.experimental.pallas import tpu as pltpu
from jax.sharding import PartitionSpec as P

GAMMA_GAS = 1.4
SMALL_EPS = 1e-06
TIME_STEP = 0.1
ROWS = 8
LANES = 128
BRICK_PARTS = 4
SUM_PARTS = 2
VMEM_BYTES = 24 * 1024 * 1024
FACE_SCALE = -TIME_STEP / 60.0
PLACE = pl.BlockSpec(memory_space=pltpu.VMEM)
ANYWHERE = pl.BlockSpec(memory_space=pl.ANY)


def call(kernel, name, micros, ins, outs, out_shape, scratch=(), aliases=None):
    return pl.pallas_call(
        kernel,
        out_shape=out_shape,
        in_specs=ins,
        out_specs=outs,
        scratch_shapes=list(scratch),
        input_output_aliases=aliases or {},
        compiler_params=pltpu.CompilerParams(vmem_limit_bytes=VMEM_BYTES),
        cost_estimate=pl.CostEstimate(
            flops=int(micros * 1e9), bytes_accessed=int(micros * 3e6), transcendentals=0
        ),
        name=name,
    )


def shape_of(*dims, dtype=jnp.float32):
    return jax.ShapeDtypeStruct(dims, dtype)


def inverse(value):
    first = pl.reciprocal(value, approx=True)
    return first * (2.0 - value * first)


def flux_of(q, normal):
    thin = inverse(q[0])
    velocity = [q[1] * thin, q[2] * thin, q[3] * thin]
    pressure = (GAMMA_GAS - 1.0) * (
        q[4] - 0.5 * (q[1] * velocity[0] + q[2] * velocity[1] + q[3] * velocity[2])
    )
    along = velocity[normal]
    flux = [q[normal + 1], q[1] * along, q[2] * along, q[3] * along, (q[4] + pressure) * along]
    flux[normal + 1] = flux[normal + 1] + pressure
    return flux, pressure, thin, along


def speed_of(pressure, thin, along):
    return jnp.abs(along) + jnp.sqrt(GAMMA_GAS * pressure * thin)


def weno_rest(d1, d2, d3, d4):
    low = d2 * d2 * 0.609375 + 3.0 * SMALL_EPS
    high = d3 * d3 * 0.609375 + 3.0 * SMALL_EPS
    x0 = d1 - 1.375 * d2
    x1 = d2 - 0.625 * d3
    x2 = d4 - 1.375 * d3
    t0 = low + x0 * x0
    t1 = high + x1 * x1
    t2 = high + x2 * x2
    w0 = t1 * t2
    w1 = t0 * t2
    w2 = t0 * t1
    w0 = w0 * w0
    w1 = w1 * w1
    w2 = w2 * w2 * 1.5
    s1 = d2 - d1
    s2 = d3 - d2
    s3 = d4 - d3
    top = w0 * (s2 - s1) + w2 * (s3 - s2)
    bottom = 0.5 * w0 + 3.0 * w1 + w2
    return top * inverse(bottom)


def face_value(dq, df, both, alpha, upwind):
    aq = [alpha * value for value in dq]
    plus = [df[k] + aq[k] for k in range(4)]
    minus = [df[k] - aq[k] for k in range(1, 5)]
    bend = df[1] - df[3]
    central = 7.0 * bend + (df[4] - df[0])
    rest = weno_rest(minus[3], minus[2], minus[1], minus[0]) - weno_rest(*plus)
    biased = 5.0 * (bend + (aq[1] + aq[3]) - (aq[2] + aq[2]) + rest)
    return 30.0 * both + jnp.where(upwind, biased, central)


def lanes(number):
    return pl.ds(pl.multiple_of(number * LANES, LANES), LANES)


def wall_kernel(low, state_ref, mask_ref, base_ref, out_ref, q_s, f_s, speed_s, dq_s, df_s):
    rows_y = state_ref.shape[2]
    width = state_ref.shape[3]
    tiles = rows_y // ROWS
    end = ROWS + rows_y
    zero = jnp.zeros((5, ROWS, LANES), jnp.float32)
    for side in (dq_s, df_s):
        side[:, 0:ROWS, :] = zero
        side[:, end : end + ROWS, :] = zero
    row = lax.broadcasted_iota(jnp.int32, (ROWS, LANES), 0)

    def column(number, carry):
        plane = number // (width // LANES)
        lane = lanes(number % (width // LANES))
        zero_row = jnp.minimum(number, 0)

        def at(r, shift):
            return pl.ds(zero_row + (r * ROWS + ROWS + shift), ROWS)

        def still(r):
            return slice(r * ROWS + ROWS, r * ROWS + 2 * ROWS)

        qs = []
        for r in range(tiles):
            mine = slice(r * ROWS, r * ROWS + ROWS)
            q = [state_ref[k, low + plane, mine, lane] for k in range(5)]
            flux, pressure, thin, along = flux_of(q, 1)
            speed = speed_of(pressure, thin, along)
            for k in range(5):
                q_s[k, still(r), :] = q[k]
                f_s[k, still(r), :] = flux[k]
            speed_s[still(r), :] = speed
            if r == 0:
                for k in range(5):
                    q_s[k, 0:ROWS, :] = jnp.broadcast_to(q[k][0:1], (ROWS, LANES))
                    f_s[k, 0:ROWS, :] = jnp.broadcast_to(flux[k][0:1], (ROWS, LANES))
                speed_s[0:ROWS, :] = jnp.broadcast_to(speed[0:1], (ROWS, LANES))
            if r == tiles - 1:
                speed_s[end : end + ROWS, :] = jnp.broadcast_to(
                    speed[ROWS - 1 : ROWS], (ROWS, LANES)
                )
        for k in range(5):
            changes = [
                (
                    q_s[k, still(r), :] - q_s[k, at(r, -1), :],
                    f_s[k, still(r), :] - f_s[k, at(r, -1), :],
                )
                for r in range(tiles)
            ]
            for r in range(tiles):
                dq_s[k, still(r), :] = changes[r][0]
                df_s[k, still(r), :] = changes[r][1]
        alphas, switches = [], []
        for r in range(tiles):
            alpha = speed_s[still(r), :]
            for shift in (-3, -2, -1, 1, 2):
                alpha = jnp.maximum(alpha, speed_s[at(r, shift), :])
            alphas.append(alpha)
            switches.append(mask_ref[low + plane, r * ROWS : r * ROWS + ROWS, lane] > 0)
        for k in range(5):
            hats = []
            for r in range(tiles):
                dq = [dq_s[k, at(r, s), :] for s in (-2, -1)]
                df = [df_s[k, at(r, s), :] for s in (-2, -1)]
                dq += [dq_s[k, still(r), :]]
                df += [df_s[k, still(r), :]]
                dq += [dq_s[k, at(r, s), :] for s in (1, 2)]
                df += [df_s[k, at(r, s), :] for s in (1, 2)]
                here = f_s[k, still(r), :]
                both = here + here - df[2]
                hats.append(face_value(dq, df, both, alphas[r], switches[r]))
            top = (
                60.0 * f_s[k, end - 1 : end, :]
                + 7.0 * df_s[k, end - 1 : end, :]
                - df_s[k, end - 2 : end - 1, :]
            )
            turned = [pltpu.roll(hat, ROWS - 1, 0) for hat in hats]
            turned.append(jnp.broadcast_to(top, (ROWS, LANES)))
            for r in range(tiles):
                after = jnp.where(row == ROWS - 1, turned[r + 1], turned[r])
                mine = slice(r * ROWS, r * ROWS + ROWS)
                out_ref[k, plane, mine, lane] = base_ref[k, low + plane, mine, lane] + FACE_SCALE * (
                    after - hats[r]
                )
        return carry

    lax.fori_loop(0, out_ref.shape[1] * (width // LANES), column, 0)


def wall_part(state, mask_y, base, low, count, after):
    fields, depth, rows_y, width = state.shape
    tall = rows_y + 2 * ROWS
    padded = pltpu.VMEM((fields, tall, LANES), jnp.float32)

    def kernel(state_ref, mask_ref, base_ref, after_ref, out_ref, *scratch):
        wall_kernel(low, state_ref, mask_ref, base_ref, out_ref, *scratch)

    return call(
        kernel,
        "wall_faces",
        5.0 * count / depth,
        [PLACE, PLACE, PLACE, ANYWHERE],
        PLACE,
        shape_of(fields, count, rows_y, width),
        [padded, padded, pltpu.VMEM((tall, LANES), jnp.float32), padded, padded],
    )(state, mask_y, base, after)


def pack_kernel(parts, state_ref, mask_ref, *refs):
    outs, (mask_s, sems) = refs[:parts], refs[parts:]
    planes, rows_all, width = state_ref.shape
    rows_y = rows_all // parts
    mask_copy = pltpu.make_async_copy(mask_ref.at[0], mask_s, sems.at[parts])
    mask_copy.start()
    copies = [
        pltpu.make_async_copy(
            state_ref.at[:, pl.ds(c * rows_y, rows_y), :], outs[c].at[pl.ds(0, planes)], sems.at[c]
        )
        for c in range(parts)
    ]
    for copy in copies:
        copy.start()
    mask_copy.wait()
    for c in range(parts):
        outs[c][planes] = mask_s[c * rows_y : (c + 1) * rows_y, :].astype(jnp.float32)
    for copy in copies:
        copy.wait()


def pack_part(state, mask_x, parts):
    fields, depth, rows_all, width = state.shape
    planes = fields * depth
    return call(
        functools.partial(pack_kernel, parts),
        "pack_bricks",
        1.0,
        [ANYWHERE, ANYWHERE],
        [PLACE] * parts,
        [shape_of(planes + 1, rows_all // parts, width)] * parts,
        [pltpu.VMEM((rows_all, width), jnp.int32), pltpu.SemaphoreType.DMA((parts + 1,))],
    )(state.reshape(planes, rows_all, width), mask_x)


def pass_kernel(depth, pair_ref, after_ref, out_ref):
    planes = pair_ref.shape[0] - 1
    skip = 1 - lax.rem(lax.axis_index("gx"), 2)
    for k in range(planes // depth):
        for i in range(3):
            out_ref[3 * k + i] = pair_ref[depth * k + i + skip * (depth - 3)]
    out_ref[3 * (planes // depth)] = pair_ref[planes]


def pass_part(pair, depth, after):
    planes, rows_y, width = pair.shape
    return call(
        functools.partial(pass_kernel, depth),
        "pass_planes",
        0.5,
        [PLACE, ANYWHERE],
        PLACE,
        shape_of(3 * (planes - 1) // depth + 1, rows_y, width),
    )(pair, after)


def stream_kernel(start, sum_start, counts, *refs):
    state_ref, pair_ref, far_ref, mask_ref, sum_ref = refs[:5]
    acc_refs = refs[5 : 5 + len(counts)]
    out_ref, dq_s, df_s, both_s, alpha_s, result, sem = refs[-7:]
    fields, depth, _, width = state_ref.shape
    rows_y = result.shape[2]
    rank = lax.axis_index("gx")
    even = lax.rem(rank, 2) == 0
    first = rank == 0
    last = rank == lax.axis_size("gx") - 1
    lane_tiles = width // LANES
    faces = depth + 1
    tiles = (rows_y // ROWS) * lane_tiles

    def place(number):
        row = (number // lane_tiles) * ROWS
        return row, lanes(number % lane_tiles)

    def rows(row, shift):
        return pl.ds(pl.multiple_of(row + shift, ROWS), ROWS)

    def point(number, carry):
        at, lane = place(number)
        row, mine = rows(at, 0), rows(at, start)
        own = [[state_ref[k, i, mine, lane] for k in range(5)] for i in range(depth)]
        cells = []
        for i in range(3):
            cells.append(
                [
                    jnp.where(
                        first,
                        own[0][k],
                        jnp.where(
                            even,
                            far_ref[3 * k + i, row, lane],
                            pair_ref[depth * k + depth - 3 + i, row, lane],
                        ),
                    )
                    for k in range(5)
                ]
            )
        cells += own
        for i in range(3):
            cells.append(
                [
                    jnp.where(
                        last,
                        own[depth - 1][k],
                        jnp.where(
                            even,
                            pair_ref[depth * k + i, row, lane],
                            far_ref[3 * k + i, row, lane],
                        ),
                    )
                    for k in range(5)
                ]
            )
        speeds, before = [], None
        for j, q in enumerate(cells):
            flux, pressure, thin, along = flux_of(q, 0)
            speeds.append(speed_of(pressure, thin, along))
            if j > 0:
                for k in range(5):
                    dq_s[number, k, j - 1] = q[k] - cells[j - 1][k]
                    df_s[number, k, j - 1] = flux[k] - before[k]
                    if 3 <= j < 3 + faces:
                        both_s[number, k, j - 3] = flux[k] + before[k]
            before = flux
        pairs = [jnp.maximum(speeds[i], speeds[i + 1]) for i in range(depth + 5)]
        for f in range(faces):
            alpha_s[number, f] = jnp.maximum(jnp.maximum(pairs[f], pairs[f + 2]), pairs[f + 4])
        return carry

    lax.fori_loop(0, tiles, point, 0)

    def faces_of(number, carry):
        at, lane = place(number)
        row, mine = rows(at, 0), rows(at, start)
        border = jnp.where(
            even, pair_ref[depth * fields, row, lane], far_ref[3 * fields, row, lane]
        )
        border = jnp.where(last, 0.0, border)
        switches = [mask_ref[i, mine, lane] > 0 for i in range(depth)] + [border > 0.0]
        results = []
        for k in range(5):
            dq = [dq_s[number, k, j] for j in range(depth + 5)]
            df = [df_s[number, k, j] for j in range(depth + 5)]
            hats = [
                face_value(
                    dq[f : f + 5], df[f : f + 5], both_s[number, k, f], alpha_s[number, f], switches[f]
                )
                for f in range(faces)
            ]
            plane = 0
            for acc_ref, count in zip(acc_refs, counts):
                for i in range(count):
                    results.append(
                        acc_ref[k, i, mine, lane]
                        - TIME_STEP * sum_ref[k, plane, rows(at, sum_start), lane]
                        + FACE_SCALE * (hats[plane + 1] - hats[plane])
                    )
                    plane += 1
        for k in range(5):
            for i in range(depth):
                result[k, i, row, lane] = results[k * depth + i]
        return carry

    lax.fori_loop(0, tiles, faces_of, 0)
    copy = pltpu.make_async_copy(result, out_ref.at[:, :, pl.ds(start, rows_y), :], sem)
    copy.start()
    copy.wait()


def stream_part(state, pair, far, mask_x, part_sum, sum_start, accs, out, start):
    fields, depth, rows_all, width = state.shape
    rows_y = pair.shape[1]
    tiles = rows_y * width // (ROWS * LANES)
    counts = [acc.shape[1] for acc in accs]
    extra = [] if out is None else [out]
    vregs = functools.partial(lambda *dims: pltpu.VMEM(dims + (ROWS, LANES), jnp.float32))
    return call(
        functools.partial(stream_kernel, start, sum_start, counts),
        "stream_faces",
        8.0 * rows_y / rows_all,
        [PLACE] * (5 + len(accs)) + [ANYWHERE] * len(extra),
        ANYWHERE,
        shape_of(*state.shape),
        [
            vregs(tiles, fields, depth + 5),
            vregs(tiles, fields, depth + 5),
            vregs(tiles, fields, depth + 1),
            vregs(tiles, depth + 1),
            pltpu.VMEM((fields, depth, rows_y, width), jnp.float32),
            pltpu.SemaphoreType.DMA,
        ],
        {5 + len(accs): 0} if extra else None,
    )(state, pair, far, mask_x, part_sum, *accs, *extra)


def circulant_tables(span):
    half = span // 2
    step = 1
    while step * step < half:
        step *= 2
    count = half // step
    places = np.arange(span)
    high = 2.0 * np.pi / span * ((np.arange(count)[:, None] * step * places[None]) % span)
    low = 2.0 * np.pi / span * ((np.arange(step)[:, None] * places[None]) % span)
    tables = np.concatenate([np.cos(high), np.sin(high), np.cos(low), np.sin(low)])
    return step, count, jnp.asarray(tables.astype(np.float32))


def circulant_kernel(count, step, scale_ref, table_ref, high_ref, low_ref, band):
    span = table_ref.shape[1]
    tall, wide = high_ref.shape
    dot = functools.partial(
        jnp.dot, precision=lax.Precision.HIGHEST, preferred_element_type=jnp.float32
    )
    inner_cos = dot(scale_ref[...], table_ref[0:count])
    inner_sin = dot(scale_ref[...], table_ref[count : 2 * count])
    low_cos = table_ref[2 * count : 2 * count + step]
    low_sin = table_ref[2 * count + step :]
    line = jnp.sum(low_sin * inner_cos + low_cos * inner_sin, axis=0, keepdims=True)
    base = jnp.broadcast_to(-line, (ROWS, span))
    place = lax.broadcasted_iota(jnp.int32, (ROWS, span), 0)
    skew = base
    for i in range(1, ROWS):
        skew = jnp.where(place == i, pltpu.roll(base, i, 1), skew)
    for b in range(LANES // ROWS):
        rows = skew if b == 0 else pltpu.roll(skew, b * ROWS, 1)
        for q in range(tall // LANES):
            at = q * LANES + b * ROWS
            first = q * LANES
            if first:
                band[at : at + ROWS, :first] = rows[:, span - first :]
            band[at : at + ROWS, first:span] = rows[:, : span - first]
    full = band[...]
    high = full.astype(jnp.bfloat16)
    low = (full - high.astype(jnp.float32)).astype(jnp.bfloat16)
    high_ref[:, :span] = high
    low_ref[:, :span] = low
    high_ref[:, span:] = high[:, : wide - span]
    low_ref[:, span:] = low[:, : wide - span]


def circulant(span_filter, span, width):
    tall = min(256, width)
    step, count, tables = circulant_tables(span)
    orders = jnp.arange(span // 2, dtype=jnp.int32).astype(jnp.float32)
    scale = 2.0 / span * (2.0 * jnp.pi / span) * orders * span_filter
    scale = scale.reshape(count, step).T
    band = shape_of(tall, span + width, dtype=jnp.bfloat16)
    return call(
        functools.partial(circulant_kernel, count, step),
        "circulant_band",
        1.0,
        [PLACE, PLACE],
        [PLACE, PLACE],
        [band, band],
        [pltpu.VMEM((tall, span), jnp.float32)],
    )(scale, tables)


def fill_lines(shards, x_refs):
    _, depth, rows_y, width = shards[0].shape
    xh, xl = x_refs
    for number, shard in enumerate(shards):

        def plane(index, carry):
            i = index // (width // LANES)
            t = index % (width // LANES)
            flux, _, _, _ = flux_of([shard[k, i, :, lanes(t)] for k in range(5)], 2)
            to = lanes(t + number * (width // LANES))
            for k in range(5):
                high = flux[k].astype(jnp.bfloat16)
                line = pl.ds(pl.multiple_of((k * depth + i) * rows_y, rows_y), rows_y)
                xh[line, to] = high
                xl[line, to] = (flux[k] - high.astype(jnp.float32)).astype(jnp.bfloat16)
            return carry

        lax.fori_loop(0, depth * (width // LANES), plane, 0)


def product(target, sources, high_ref, low_ref, xh, xl, w_s):
    tall, wide = high_ref.shape
    width = xh.shape[1] // len(sources)
    span = wide - width
    deep = xh.shape[1]
    for number, source in enumerate(sources):
        for q in range(width // tall):
            start = lax.rem((target - source) * width - q * tall + 2 * span, span)
            start = pl.multiple_of(start, LANES)
            at = number * width + q * tall
            w_s[at : at + tall, :] = high_ref[:, pl.ds(start, width)]
            w_s[deep + at : deep + at + tall, :] = low_ref[:, pl.ds(start, width)]
    dot = functools.partial(jnp.dot, preferred_element_type=jnp.float32)
    high = w_s[:deep, :]
    return dot(xh[...], high) + dot(xl[...], high) + dot(xh[...], w_s[deep:, :])


def away_kernel(masks, parts, high_ref, low_ref, own_ref, core_ref, after_ref, *refs):
    sums = refs[: len(masks) * parts]
    xh, xl, w_s = refs[len(masks) * parts :]
    fields, depth, rows_all, width = own_ref.shape
    rows_y = rows_all // parts
    me = lax.axis_index("gz")
    fill_lines([own_ref, core_ref], [xh, xl])
    for number, mask in enumerate(masks):
        total = product(me ^ mask, [me, me ^ 1], high_ref, low_ref, xh, xl, w_s)
        total = total.reshape(fields, depth, rows_all, width)
        for c in range(parts):
            sums[number * parts + c][...] = total[:, :, c * rows_y : (c + 1) * rows_y, :]


def away_part(band, state, core, masks, parts, after):
    fields, depth, rows_all, width = state.shape
    lines = fields * depth * rows_all
    line = shape_of(lines, 2 * width, dtype=jnp.bfloat16)
    count = len(masks) * parts
    outs = call(
        functools.partial(away_kernel, masks, parts),
        "span_away",
        3.0,
        [PLACE] * 4 + [ANYWHERE],
        [PLACE] * (count + 2),
        [shape_of(fields, depth, rows_all // parts, width)] * count + [line, line],
        [pltpu.VMEM((4 * width, width), jnp.bfloat16)],
    )(*band, state, core, after)
    return outs[:count], outs[count:]


def home_kernel(high_ref, low_ref, xh, xl, state_ref, out_ref, w_s):
    me = lax.axis_index("gz")
    total = product(me, [me, me ^ 1], high_ref, low_ref, xh, xl, w_s)
    out_ref[...] = state_ref[...] - TIME_STEP * total.reshape(state_ref.shape)


def home_part(band, lines, state):
    width = state.shape[3]
    return call(
        home_kernel,
        "span_home",
        2.0,
        [PLACE] * 5,
        PLACE,
        shape_of(*state.shape),
        [pltpu.VMEM((4 * width, width), jnp.bfloat16)],
    )(*band, *lines, state)


def per_device(state, mask_x, mask_y, span_filter):
    fields, depth, rows_all, width = state.shape
    groups = lax.axis_size("gz")
    slabs = lax.axis_size("gx")
    span = width * groups

    def flip(array, bit):
        return lax.ppermute(array, "gz", [(g, g ^ bit) for g in range(groups)])

    swap = [(i, i ^ 1) for i in range(slabs)]
    carry = [(i, i + 2) for i in range(0, slabs - 2, 2)] + [
        (i, i - 2) for i in range(3, slabs, 2)
    ]
    core = flip(state, 1)
    bricks = pack_part(state, mask_x, BRICK_PARTS)
    pairs = [lax.ppermute(brick, "gx", swap) for brick in bricks]
    band = circulant(span_filter, span, width)

    masks = list(range(2, groups, 2))
    sums, lines = away_part(band, state, core, masks, SUM_PARTS, bricks[0])
    arrived = [
        sum(
            flip(sums[n * SUM_PARTS + c], mask) for n, mask in enumerate(masks)
        )
        for c in range(SUM_PARTS)
    ]
    half = depth // 2
    fars = []

    def hand_on(c, after):
        fars.append(lax.ppermute(pass_part(pairs[c], depth, after), "gx", carry))

    hand_on(0, lines[0])
    base = home_part(band, lines, state)
    acc_low = wall_part(state, mask_y, base, 0, half, lines[0])
    hand_on(1, acc_low)
    acc_high = wall_part(state, mask_y, base, half, depth - half, acc_low)
    for c in range(2, BRICK_PARTS):
        hand_on(c, acc_high)

    out = None
    step = rows_all // BRICK_PARTS
    wide = rows_all // SUM_PARTS
    for c in range(BRICK_PARTS):
        out = stream_part(
            state,
            pairs[c],
            fars[c],
            mask_x,
            arrived[c * step // wide],
            c * step % wide,
            [acc_low, acc_high],
            out,
            c * step,
        )
    return out


def solution(mesh):
    return jax.shard_map(
        per_device,
        mesh=mesh,
        in_specs=(P(None, "gx", None, "gz"), P("gx", None, "gz"), P("gx", None, "gz"), P()),
        out_specs=P(None, "gx", None, "gz"),
        check_vma=False,
    )
```

profile of v0, /device:TPU:0, one launch (start us, length us, event | category | flops | bytes accessed | tf_op | source)
XLA Modules:
  0.0 55.6 jit_solution(5738696520371947968)
XLA Ops:
  0.0 0.5 collective-permute-start.1
  0.5 0.0 copy-start
  0.5 1.3 %copy-done = f32[5,4,32,512]{3,2,1,0:T(8,128)S(1)} copy-done((f32[5,4,32,512]{3,2,1,0:T(8,128)S(1)}, f32[5,4,32,512]{3,2,1,0:T(8,128)}, u32[]{:S(2)}) %copy-start) | copy-done | bytes 1310744
  1.8 0.0 copy-start.3
  1.8 0.9 %copy-done.3 = s32[4,32,512]{2,1,0:T(8,128)S(1)} copy-done((s32[4,32,512]{2,1,0:T(8,128)S(1)}, s32[4,32,512]{2,1,0:T(8,128)}, u32[]{:S(2)}) %copy-start.3) | copy-done | bytes 262168
  2.7 0.0 copy-start.6
  2.7 1.1 %pack_bricks.1 = (f32[21,8,512]{2,1,0:T(8,128)}, f32[21,8,512]{2,1,0:T(8,128)}, f32[21,8,512]{2,1,0:T(8,128)S(1)}, f32[21,8,512]{2,1,0:T(8,128)S(1)}) custom-call(f32[20,32,512]{2,1,0:T(8,128)S(1)} %bitcast.2, s32[4,32,512]{2,1,0:T(8,128)S(1)} %copy-done.3), custom_call_target="tpu_custom_call" | custom-call | flops 1000000000 | bytes 3000000 | tf_op jit(solution)/shard_map/pack_bricks/pallas_call | solution.py:235
  3.8 2.6 %collective-permute-start.9 = (f32[21,8,512]{2,1,0:T(8,128)}, f32[21,8,512]{2,1,0:T(8,128)S(1)}, u32[]{:S(2)}, u32[]{:S(2)}) collective-permute-start(f32[21,8,512]{2,1,0:T(8,128)} %get-tuple-element.18.after_ref), channel_id=1, source_target_pairs={{0,4},{4,0},{8,12},{12,8},{16,20},{20,16},{24,28},{28,24},{1,5},{5... | collective-permute-start | bytes 1032200 | tf_op jit(solution)/shard_map/ppermute | solution.py:572
  6.3 0.1 collective-permute-start.6
  6.4 1.9 %collective-permute-start.4 = (f32[21,8,512]{2,1,0:T(8,128)S(1)}, f32[21,8,512]{2,1,0:T(8,128)S(1)}, u32[]{:S(2)}, u32[]{:S(2)}) collective-permute-start(f32[21,8,512]{2,1,0:T(8,128)S(1)} %get-tuple-element.22), channel_id=1, source_target_pairs={{0,4},{4,0},{8,12},{12,8},{16,20},{20,16},{24,28},{28,24},{1,5},{5... | collective-permute-start | bytes 1032200 | tf_op jit(solution)/shard_map/ppermute | solution.py:572
  8.4 0.1 collective-permute-start
  8.4 0.0 copy-done.6
  8.5 0.1 reshape.7
  8.5 0.1 copy.9
  8.6 0.0 copy-start.5
  8.6 1.2 %copy-done.5 = f32[128,2048]{1,0:T(8,128)S(1)} copy-done((f32[128,2048]{1,0:T(8,128)S(1)}, f32[128,2048]{1,0:T(8,128)}, u32[]{:S(2)}) %copy-start.5) | copy-done | bytes 1048600
  9.8 0.0 copy-start.1
  9.8 0.9 %circulant_band.1 = (bf16[256,2560]{1,0:T(8,128)(2,1)S(1)}, bf16[256,2560]{1,0:T(8,128)(2,1)S(1)}) custom-call(f32[32,32]{1,0:T(8,128)S(1)} %bitcast.3, f32[128,2048]{1,0:T(8,128)S(1)} %copy-done.5), custom_call_target="tpu_custom_call" | custom-call | flops 1000000000 | bytes 3000000 | tf_op jit(solution)/shard_map/circulant_band/pallas_call | solution.py:459
  10.8 0.0 collective-permute-done.1.core_ref
  10.8 0.4 copy-done.1
  11.2 3.5 %span_away.1 = (f32[5,4,16,512]{3,2,1,0:T(8,128)S(1)}, f32[5,4,16,512]{3,2,1,0:T(8,128)S(1)}, bf16[640,1024]{1,0:T(8,128)(2,1)S(1)}, bf16[640,1024]{1,0:T(8,128)(2,1)S(1)}) custom-call(bf16[256,2560]{1,0:T(8,128)(2,1)S(1)} %get-tuple-element.16.high_ref, bf16[256,2560]{1,0:T(8,128)(2,1)S(1)} %get-tuple-element.17.low_ref, f32[5,4,32,512]{3,2,1,0:T(8,128)S(1)} %copy-done.1, ...), custom_call_target="tpu_custom_call" | custom-call | flops 3000000000 | bytes 9000000 | tf_op jit(solution)/shard_map/span_away/pallas_call | solution.py:526
  14.7 2.0 %collective-permute-start.8 = (f32[5,4,16,512]{3,2,1,0:T(8,128)S(1)}, f32[5,4,16,512]{3,2,1,0:T(8,128)S(1)}, u32[]{:S(2)}, u32[]{:S(2)}) collective-permute-start(f32[5,4,16,512]{3,2,1,0:T(8,128)S(1)} %get-tuple-element.24), channel_id=1, source_target_pairs={{0,2},{1,3},{2,0},{3,1},{4,6},{5,7},{6,4},{7,5},{8,10},{9,11},{10,... | collective-permute-start | bytes 1966088 | tf_op jit(solution)/shard_map/ppermute | solution.py:564
  16.7 2.2 %span_home.1.base_ref = f32[5,4,32,512]{3,2,1,0:T(8,128)S(1)} custom-call(bf16[256,2560]{1,0:T(8,128)(2,1)S(1)} %get-tuple-element.16.high_ref, bf16[256,2560]{1,0:T(8,128)(2,1)S(1)} %get-tuple-element.17.low_ref, bf16[640,1024]{1,0:T(8,128)(2,1)S(1)} %get-tuple-element.19.xh.after_ref, bf16[640,1024]{1,0:T(8,128)(2,1)S(1)} %get-tuple-element.20.xl, ...), custom_call_target="tpu_custom_call" | custom-call | flops 2000000000 | bytes 6000000 | tf_op jit(solution)/shard_map/span_home/pallas_call | solution.py:546
  18.9 0.0 copy-start.2
  18.9 0.0 collective-permute-done.9.pair_ref.refs_1_
  19.0 3.6 %collective-permute-start.10 = (f32[16,8,512]{2,1,0:T(8,128)S(1)}, f32[16,8,512]{2,1,0:T(8,128)S(1)}, u32[]{:S(2)}, u32[]{:S(2)}) collective-permute-start(f32[16,8,512]{2,1,0:T(8,128)S(1)} %pass_planes.7), channel_id=1, source_target_pairs={{0,8},{8,16},{16,24},{12,4},{20,12},{28,20},{1,9},{9,17},{17,25},{... | collective-permute-start | bytes 786440 | tf_op jit(solution)/shard_map/ppermute | solution.py:587
  22.6 0.0 copy-done.2
  22.6 3.1 %wall_faces.2.after_ref.refs_5_ = f32[5,2,32,512]{3,2,1,0:T(8,128)S(1)} custom-call(f32[5,4,32,512]{3,2,1,0:T(8,128)S(1)} %copy-done.1, s32[4,32,512]{2,1,0:T(8,128)S(1)} %copy-done.2, f32[5,4,32,512]{3,2,1,0:T(8,128)S(1)} %span_home.1.base_ref, bf16[640,1024]{1,0:T(8,128)(2,1)S(1)} %get-tuple-element.19.xh.after_ref), custom_call_target="tpu_custom_call" | custom-call | flops 2500000000 | bytes 7500000 | tf_op jit(solution)/shard_map/wall_faces/pallas_call | solution.py:200
  25.7 0.0 collective-permute-done.6.pair_ref.refs_1_
  25.8 0.6 %collective-permute-start.3 = (f32[5,4,16,512]{3,2,1,0:T(8,128)S(1)}, f32[5,4,16,512]{3,2,1,0:T(8,128)S(1)}, u32[]{:S(2)}, u32[]{:S(2)}) collective-permute-start(f32[5,4,16,512]{3,2,1,0:T(8,128)S(1)} %get-tuple-element.21), channel_id=1, source_target_pairs={{0,2},{1,3},{2,0},{3,1},{4,6},{5,7},{6,4},{7,5},{8,10},{9,11},{10,... | collective-permute-start | bytes 1966088 | tf_op jit(solution)/shard_map/ppermute | solution.py:564
  26.4 3.1 %wall_faces.3.after_ref.refs_6_ = f32[5,2,32,512]{3,2,1,0:T(8,128)S(1)} custom-call(f32[5,4,32,512]{3,2,1,0:T(8,128)S(1)} %copy-done.1, s32[4,32,512]{2,1,0:T(8,128)S(1)} %copy-done.2, f32[5,4,32,512]{3,2,1,0:T(8,128)S(1)} %span_home.1.base_ref, f32[5,2,32,512]{3,2,1,0:T(8,128)S(1)} %wall_faces.2.after_ref.refs_5_), custom_call_target="tpu_custom_call" | custom-call | flops 2500000000 | bytes 7500000 | tf_op jit(solution)/shard_map/wall_faces/pallas_call | solution.py:200
  29.5 0.7 %collective-permute-done.4.pair_ref.refs_1_ = f32[21,8,512]{2,1,0:T(8,128)S(1)} collective-permute-done((f32[21,8,512]{2,1,0:T(8,128)S(1)}, f32[21,8,512]{2,1,0:T(8,128)S(1)}, u32[]{:S(2)}, u32[]{:S(2)}) %collective-permute-start.4) | collective-permute-done | bytes 344096 | tf_op jit(solution)/shard_map/ppermute | solution.py:572
  30.2 3.9 %collective-permute-start.7 = (f32[16,8,512]{2,1,0:T(8,128)S(1)}, f32[16,8,512]{2,1,0:T(8,128)S(1)}, u32[]{:S(2)}, u32[]{:S(2)}) collective-permute-start(f32[16,8,512]{2,1,0:T(8,128)S(1)} %pass_planes.6), channel_id=1, source_target_pairs={{0,8},{8,16},{16,24},{12,4},{20,12},{28,20},{1,9},{9,17},{17,25},{... | collective-permute-start | bytes 786440 | tf_op jit(solution)/shard_map/ppermute | solution.py:587
  34.2 0.0 copy-start.4
  34.2 3.2 %collective-permute-done.pair_ref.refs_1_ = f32[21,8,512]{2,1,0:T(8,128)S(1)} collective-permute-done((f32[21,8,512]{2,1,0:T(8,128)S(1)}, f32[21,8,512]{2,1,0:T(8,128)S(1)}, u32[]{:S(2)}, u32[]{:S(2)}) %collective-permute-start) | collective-permute-done | bytes 344096 | tf_op jit(solution)/shard_map/ppermute | solution.py:572
  37.4 3.7 %collective-permute-start.5 = (f32[16,8,512]{2,1,0:T(8,128)S(1)}, f32[16,8,512]{2,1,0:T(8,128)S(1)}, u32[]{:S(2)}, u32[]{:S(2)}) collective-permute-start(f32[16,8,512]{2,1,0:T(8,128)S(1)} %pass_planes.5), channel_id=1, source_target_pairs={{0,8},{8,16},{16,24},{12,4},{20,12},{28,20},{1,9},{9,17},{17,25},{... | collective-permute-start | bytes 786440 | tf_op jit(solution)/shard_map/ppermute | solution.py:587
  41.2 0.0 collective-permute-done.10.refs_2_
  41.2 3.5 %collective-permute-start.2 = (f32[16,8,512]{2,1,0:T(8,128)S(1)}, f32[16,8,512]{2,1,0:T(8,128)S(1)}, u32[]{:S(2)}, u32[]{:S(2)}) collective-permute-start(f32[16,8,512]{2,1,0:T(8,128)S(1)} %pass_planes.4), channel_id=1, source_target_pairs={{0,8},{8,16},{16,24},{12,4},{20,12},{28,20},{1,9},{9,17},{17,25},{... | collective-permute-start | bytes 786440 | tf_op jit(solution)/shard_map/ppermute | solution.py:587
  44.7 0.0 collective-permute-done.8.refs_4_
  44.7 0.0 copy-done.4
  44.7 2.7 %stream_faces.4.refs_7_ = f32[5,4,32,512]{3,2,1,0:T(8,128)} custom-call(f32[5,4,32,512]{3,2,1,0:T(8,128)S(1)} %copy-done.1, f32[21,8,512]{2,1,0:T(8,128)S(1)} %collective-permute-done.9.pair_ref.refs_1_, f32[16,8,512]{2,1,0:T(8,128)S(1)} %collective-permute-done.10.refs_2_, s32[4,32,512]{2,1,0:T(8,128)S(1)} %copy-done.4, ...), custom_call_target="tpu_custom_call" | custom-call | flops 2000000000 | bytes 6000000 | tf_op jit(solution)/shard_map/stream_faces/pallas_call | solution.py:387
  47.4 0.0 collective-permute-done.7.refs_2_
  47.4 2.7 %stream_faces.5.refs_7_ = f32[5,4,32,512]{3,2,1,0:T(8,128)} custom-call(f32[5,4,32,512]{3,2,1,0:T(8,128)S(1)} %copy-done.1, f32[21,8,512]{2,1,0:T(8,128)S(1)} %collective-permute-done.6.pair_ref.refs_1_, f32[16,8,512]{2,1,0:T(8,128)S(1)} %collective-permute-done.7.refs_2_, s32[4,32,512]{2,1,0:T(8,128)S(1)} %copy-done.4, ...), custom_call_target="tpu_custom_call", output_to_operand_aliasing={{}: (7, {})} | custom-call | flops 2000000000 | bytes 6000000 | tf_op jit(solution)/shard_map/stream_faces/pallas_call | solution.py:387
  50.1 0.0 collective-permute-done.5.refs_2_
  50.2 0.0 collective-permute-done.3.refs_4_
  50.2 2.7 %stream_faces.6.refs_7_ = f32[5,4,32,512]{3,2,1,0:T(8,128)} custom-call(f32[5,4,32,512]{3,2,1,0:T(8,128)S(1)} %copy-done.1, f32[21,8,512]{2,1,0:T(8,128)S(1)} %collective-permute-done.4.pair_ref.refs_1_, f32[16,8,512]{2,1,0:T(8,128)S(1)} %collective-permute-done.5.refs_2_, s32[4,32,512]{2,1,0:T(8,128)S(1)} %copy-done.4, ...), custom_call_target="tpu_custom_call", output_to_operand_aliasing={{}: (7, {})} | custom-call | flops 2000000000 | bytes 6000000 | tf_op jit(solution)/shard_map/stream_faces/pallas_call | solution.py:387
  52.9 0.0 collective-permute-done.2.refs_2_
  52.9 2.7 %stream_faces.7 = f32[5,4,32,512]{3,2,1,0:T(8,128)} custom-call(f32[5,4,32,512]{3,2,1,0:T(8,128)S(1)} %copy-done.1, f32[21,8,512]{2,1,0:T(8,128)S(1)} %collective-permute-done.pair_ref.refs_1_, f32[16,8,512]{2,1,0:T(8,128)S(1)} %collective-permute-done.2.refs_2_, s32[4,32,512]{2,1,0:T(8,128)S(1)} %copy-done.4, ...), custom_call_target="tpu_custom_call", output_to_operand_aliasing={{}: (7, {})} | custom-call | flops 2000000000 | bytes 6000000 | tf_op jit(solution)/shard_map/stream_faces/pallas_call | solution.py:387
  (5 shorter events, 0.1 us)
Async XLA Ops:
  0.0 10.8 %collective-permute-start.1 = (f32[5,4,32,512]{3,2,1,0:T(8,128)}, f32[5,4,32,512]{3,2,1,0:T(8,128)S(1)}, u32[]{:S(2)}, u32[]{:S(2)}) collective-permute-start(f32[5,4,32,512]{3,2,1,0:T(8,128)} %refs_0_.7), channel_id=1, source_target_pairs={{0,1},{1,0},{2,3},{3,2},{4,5},{5,4},{6,7},{7,6},{8,9},{9,8},{10,11... | collective-permute-start | bytes 3932168 | tf_op jit(solution)/shard_map/ppermute | solution.py:564
  0.5 1.3 %copy-start = (f32[5,4,32,512]{3,2,1,0:T(8,128)S(1)}, f32[5,4,32,512]{3,2,1,0:T(8,128)}, u32[]{:S(2)}) copy-start(f32[5,4,32,512]{3,2,1,0:T(8,128)} %refs_0_.7) | copy-start | bytes 3932164
  1.8 0.9 %copy-start.3 = (s32[4,32,512]{2,1,0:T(8,128)S(1)}, s32[4,32,512]{2,1,0:T(8,128)}, u32[]{:S(2)}) copy-start(s32[4,32,512]{2,1,0:T(8,128)} %refs_3_.7) | copy-start | bytes 786436
  2.7 5.7 %copy-start.6 = (f32[1024]{0:T(1024)S(1)}, f32[1024]{0:T(1024)}, u32[]{:S(2)}) copy-start(f32[1024]{0:T(1024)} %param.8) | copy-start | bytes 12292
  3.8 15.1 %collective-permute-start.9 = (f32[21,8,512]{2,1,0:T(8,128)}, f32[21,8,512]{2,1,0:T(8,128)S(1)}, u32[]{:S(2)}, u32[]{:S(2)}) collective-permute-start(f32[21,8,512]{2,1,0:T(8,128)} %get-tuple-element.18.after_ref), channel_id=1, source_target_pairs={{0,4},{4,0},{8,12},{12,8},{16,20},{20,16},{24,28},{28,24},{1,5},{5... | collective-permute-start | bytes 1032200 | tf_op jit(solution)/shard_map/ppermute | solution.py:572
  6.3 19.4 %collective-permute-start.6 = (f32[21,8,512]{2,1,0:T(8,128)}, f32[21,8,512]{2,1,0:T(8,128)S(1)}, u32[]{:S(2)}, u32[]{:S(2)}) collective-permute-start(f32[21,8,512]{2,1,0:T(8,128)} %get-tuple-element.23), channel_id=1, source_target_pairs={{0,4},{4,0},{8,12},{12,8},{16,20},{20,16},{24,28},{28,24},{1,5},{5... | collective-permute-start | bytes 1032200 | tf_op jit(solution)/shard_map/ppermute | solution.py:572
  6.4 23.8 %collective-permute-start.4 = (f32[21,8,512]{2,1,0:T(8,128)S(1)}, f32[21,8,512]{2,1,0:T(8,128)S(1)}, u32[]{:S(2)}, u32[]{:S(2)}) collective-permute-start(f32[21,8,512]{2,1,0:T(8,128)S(1)} %get-tuple-element.22), channel_id=1, source_target_pairs={{0,4},{4,0},{8,12},{12,8},{16,20},{20,16},{24,28},{28,24},{1,5},{5... | collective-permute-start | bytes 1032200 | tf_op jit(solution)/shard_map/ppermute | solution.py:572
  8.4 29.0 %collective-permute-start = (f32[21,8,512]{2,1,0:T(8,128)S(1)}, f32[21,8,512]{2,1,0:T(8,128)S(1)}, u32[]{:S(2)}, u32[]{:S(2)}) collective-permute-start(f32[21,8,512]{2,1,0:T(8,128)S(1)} %get-tuple-element.15), channel_id=1, source_target_pairs={{0,4},{4,0},{8,12},{12,8},{16,20},{20,16},{24,28},{28,24},{1,5},{5... | collective-permute-start | bytes 1032200 | tf_op jit(solution)/shard_map/ppermute | solution.py:572
  8.6 1.2 %copy-start.5 = (f32[128,2048]{1,0:T(8,128)S(1)}, f32[128,2048]{1,0:T(8,128)}, u32[]{:S(2)}) copy-start(f32[128,2048]{1,0:T(8,128)} %constant.4.clone.table_ref) | copy-start | bytes 3145732
  9.8 1.3 %copy-start.1 = (f32[5,4,32,512]{3,2,1,0:T(8,128)S(1)}, f32[5,4,32,512]{3,2,1,0:T(8,128)}, u32[]{:S(2)}) copy-start(f32[5,4,32,512]{3,2,1,0:T(8,128)} %refs_0_.7) | copy-start | bytes 3932164
  14.7 30.0 %collective-permute-start.8 = (f32[5,4,16,512]{3,2,1,0:T(8,128)S(1)}, f32[5,4,16,512]{3,2,1,0:T(8,128)S(1)}, u32[]{:S(2)}, u32[]{:S(2)}) collective-permute-start(f32[5,4,16,512]{3,2,1,0:T(8,128)S(1)} %get-tuple-element.24), channel_id=1, source_target_pairs={{0,2},{1,3},{2,0},{3,1},{4,6},{5,7},{6,4},{7,5},{8,10},{9,11},{10,... | collective-permute-start | bytes 1966088 | tf_op jit(solution)/shard_map/ppermute | solution.py:564
  18.9 3.7 %copy-start.2 = (s32[4,32,512]{2,1,0:T(8,128)S(1)}, s32[4,32,512]{2,1,0:T(8,128)}, u32[]{:S(2)}) copy-start(s32[4,32,512]{2,1,0:T(8,128)} %mask_ref.5) | copy-start | bytes 786436
  19.0 22.2 %collective-permute-start.10 = (f32[16,8,512]{2,1,0:T(8,128)S(1)}, f32[16,8,512]{2,1,0:T(8,128)S(1)}, u32[]{:S(2)}, u32[]{:S(2)}) collective-permute-start(f32[16,8,512]{2,1,0:T(8,128)S(1)} %pass_planes.7), channel_id=1, source_target_pairs={{0,8},{8,16},{16,24},{12,4},{20,12},{28,20},{1,9},{9,17},{17,25},{... | collective-permute-start | bytes 786440 | tf_op jit(solution)/shard_map/ppermute | solution.py:587
  25.8 24.4 %collective-permute-start.3 = (f32[5,4,16,512]{3,2,1,0:T(8,128)S(1)}, f32[5,4,16,512]{3,2,1,0:T(8,128)S(1)}, u32[]{:S(2)}, u32[]{:S(2)}) collective-permute-start(f32[5,4,16,512]{3,2,1,0:T(8,128)S(1)} %get-tuple-element.21), channel_id=1, source_target_pairs={{0,2},{1,3},{2,0},{3,1},{4,6},{5,7},{6,4},{7,5},{8,10},{9,11},{10,... | collective-permute-start | bytes 1966088 | tf_op jit(solution)/shard_map/ppermute | solution.py:564
  30.2 17.2 %collective-permute-start.7 = (f32[16,8,512]{2,1,0:T(8,128)S(1)}, f32[16,8,512]{2,1,0:T(8,128)S(1)}, u32[]{:S(2)}, u32[]{:S(2)}) collective-permute-start(f32[16,8,512]{2,1,0:T(8,128)S(1)} %pass_planes.6), channel_id=1, source_target_pairs={{0,8},{8,16},{16,24},{12,4},{20,12},{28,20},{1,9},{9,17},{17,25},{... | collective-permute-start | bytes 786440 | tf_op jit(solution)/shard_map/ppermute | solution.py:587
  34.2 10.5 %copy-start.4 = (s32[4,32,512]{2,1,0:T(8,128)S(1)}, s32[4,32,512]{2,1,0:T(8,128)}, u32[]{:S(2)}) copy-start(s32[4,32,512]{2,1,0:T(8,128)} %refs_3_.7) | copy-start | bytes 786436
  37.4 12.7 %collective-permute-start.5 = (f32[16,8,512]{2,1,0:T(8,128)S(1)}, f32[16,8,512]{2,1,0:T(8,128)S(1)}, u32[]{:S(2)}, u32[]{:S(2)}) collective-permute-start(f32[16,8,512]{2,1,0:T(8,128)S(1)} %pass_planes.5), channel_id=1, source_target_pairs={{0,8},{8,16},{16,24},{12,4},{20,12},{28,20},{1,9},{9,17},{17,25},{... | collective-permute-start | bytes 786440 | tf_op jit(solution)/shard_map/ppermute | solution.py:587
  41.2 11.7 %collective-permute-start.2 = (f32[16,8,512]{2,1,0:T(8,128)S(1)}, f32[16,8,512]{2,1,0:T(8,128)S(1)}, u32[]{:S(2)}, u32[]{:S(2)}) collective-permute-start(f32[16,8,512]{2,1,0:T(8,128)S(1)} %pass_planes.4), channel_id=1, source_target_pairs={{0,8},{8,16},{16,24},{12,4},{20,12},{28,20},{1,9},{9,17},{17,25},{... | collective-permute-start | bytes 786440 | tf_op jit(solution)/shard_map/ppermute | solution.py:587
where the time goes:
time: 55.9 us; the launch traced here: 55.6 us
  Pallas kernels  24.9 us (45%)
  starting transfers between devices  22.5 us (40%)
  local copies, waits for them, and re-layouts  4.04 us (7%)
  waiting for transfers between devices  3.94 us (7%)
    ppermute x4, starting transfers between devices, hand_on(): fars.append(lax.ppermute(pass_part(pairs[c], depth, after), 'gx', carry))  14.8 us
    pallas_call x4, Pallas kernels, stream_part(): call(functools.partial(stream_kernel, start, sum_start, counts), 'stream_...  10.8 us
    pallas_call x2, Pallas kernels, wall_part(): call(kernel, 'wall_faces', 5.0 * count / depth, [PLACE, PLACE, PLACE, ANY...  6.28 us
    ppermute x4, starting transfers between devices, per_device(): pairs = [lax.ppermute(brick, 'gx', swap) for brick in bricks]  4.66 us
    ppermute x4, waiting for transfers between devices, per_device(): pairs = [lax.ppermute(brick, 'gx', swap) for brick in bricks]  3.92 us
    unnamed x14, local copies, waits for them, and re-layouts  3.9 us
    pallas_call x1, Pallas kernels, away_part(): call(functools.partial(away_kernel, masks, parts), 'span_away', 3.0, [PLA...  3.5 us
    ppermute x3, starting transfers between devices, flip(): return lax.ppermute(array, 'gz', [(g, g ^ bit) for g in range(groups)])  3.07 us
  transfers between devices with their start and end apart: 11, of which 2 were waited for; matrix products, arithmetic and copies ran while one was open for 0% of the time, Pallas kernels for 40%

commit v1 on v0

--- a/solution.py
+++ b/solution.py
@@ -13,15 +13,16 @@
 TIME_STEP = 0.1
 ROWS = 8
 LANES = 128
-BRICK_PARTS = 4
+BRICK_PARTS = (2, 1, 1)
 SUM_PARTS = 2
 VMEM_BYTES = 24 * 1024 * 1024
 FACE_SCALE = -TIME_STEP / 60.0
 PLACE = pl.BlockSpec(memory_space=pltpu.VMEM)
 ANYWHERE = pl.BlockSpec(memory_space=pl.ANY)
-
-
-def call(kernel, name, micros, ins, outs, out_shape, scratch=(), aliases=None):
+HBM = pl.BlockSpec(memory_space=pltpu.HBM)
+
+
+def call(kernel, name, weight, ins, outs, out_shape, scratch=(), aliases=None):
     return pl.pallas_call(
         kernel,
         out_shape=out_shape,
@@ -31,7 +32,7 @@
         input_output_aliases=aliases or {},
         compiler_params=pltpu.CompilerParams(vmem_limit_bytes=VMEM_BYTES),
         cost_estimate=pl.CostEstimate(
-            flops=int(micros * 1e9), bytes_accessed=int(micros * 3e6), transcendentals=0
+            flops=int(weight * 1e8), bytes_accessed=int(weight * 3e5), transcendentals=0
         ),
         name=name,
     )
@@ -77,12 +78,9 @@
     w0 = w0 * w0
     w1 = w1 * w1
     w2 = w2 * w2 * 1.5
-    s1 = d2 - d1
-    s2 = d3 - d2
-    s3 = d4 - d3
-    top = w0 * (s2 - s1) + w2 * (s3 - s2)
+    top = w0 * (x0 + (d3 - 0.625 * d2)) + w2 * (x1 + x2)
     bottom = 0.5 * w0 + 3.0 * w1 + w2
-    return top * inverse(bottom)
+    return top * pl.reciprocal(bottom, approx=True)
 
 
 def face_value(dq, df, both, alpha, upwind):
@@ -208,25 +206,16 @@
     )(state, mask_y, base, after)
 
 
-def pack_kernel(parts, state_ref, mask_ref, *refs):
-    outs, (mask_s, sems) = refs[:parts], refs[parts:]
-    planes, rows_all, width = state_ref.shape
-    rows_y = rows_all // parts
-    mask_copy = pltpu.make_async_copy(mask_ref.at[0], mask_s, sems.at[parts])
-    mask_copy.start()
-    copies = [
-        pltpu.make_async_copy(
-            state_ref.at[:, pl.ds(c * rows_y, rows_y), :], outs[c].at[pl.ds(0, planes)], sems.at[c]
-        )
-        for c in range(parts)
-    ]
-    for copy in copies:
-        copy.start()
-    mask_copy.wait()
-    for c in range(parts):
-        outs[c][planes] = mask_s[c * rows_y : (c + 1) * rows_y, :].astype(jnp.float32)
-    for copy in copies:
-        copy.wait()
+def pack_kernel(parts, state_ref, mask_ref, *outs):
+    planes = state_ref.shape[0]
+    for (start, rows), out in zip(parts, outs):
+
+        def plane(index, carry):
+            out[index] = state_ref[index, start : start + rows, :]
+            return carry
+
+        lax.fori_loop(0, planes, plane, 0, unroll=2)
+        out[planes] = mask_ref[start : start + rows, :].astype(jnp.float32)
 
 
 def pack_part(state, mask_x, parts):
@@ -235,12 +224,11 @@
     return call(
         functools.partial(pack_kernel, parts),
         "pack_bricks",
-        1.0,
-        [ANYWHERE, ANYWHERE],
-        [PLACE] * parts,
-        [shape_of(planes + 1, rows_all // parts, width)] * parts,
-        [pltpu.VMEM((rows_all, width), jnp.int32), pltpu.SemaphoreType.DMA((parts + 1,))],
-    )(state.reshape(planes, rows_all, width), mask_x)
+        0.5,
+        [PLACE, PLACE],
+        [PLACE] * len(parts),
+        [shape_of(planes + 1, rows, width) for _, rows in parts],
+    )(state.reshape(planes, rows_all, width), mask_x[0])
 
 
 def pass_kernel(depth, pair_ref, after_ref, out_ref):
@@ -369,12 +357,21 @@
         for k in range(5):
             for i in range(depth):
                 result[k, i, row, lane] = results[k * depth + i]
+        hand_out(number).start()
         return carry
 
+    def hand_out(number):
+        at, lane = place(number)
+        return pltpu.make_async_copy(
+            result.at[:, :, rows(at, 0), lane], out_ref.at[:, :, rows(at, start), lane], sem.at[number]
+        )
+
+    def settle(number, carry):
+        hand_out(number).wait()
+        return carry
+
     lax.fori_loop(0, tiles, faces_of, 0)
-    copy = pltpu.make_async_copy(result, out_ref.at[:, :, pl.ds(start, rows_y), :], sem)
-    copy.start()
-    copy.wait()
+    lax.fori_loop(0, tiles, settle, 0)
 
 
 def stream_part(state, pair, far, mask_x, part_sum, sum_start, accs, out, start):
@@ -388,8 +385,8 @@
         functools.partial(stream_kernel, start, sum_start, counts),
         "stream_faces",
         8.0 * rows_y / rows_all,
-        [PLACE] * (5 + len(accs)) + [ANYWHERE] * len(extra),
-        ANYWHERE,
+        [PLACE] * (5 + len(accs)) + [HBM] * len(extra),
+        HBM,
         shape_of(*state.shape),
         [
             vregs(tiles, fields, depth + 5),
@@ -397,7 +394,7 @@
             vregs(tiles, fields, depth + 1),
             vregs(tiles, depth + 1),
             pltpu.VMEM((fields, depth, rows_y, width), jnp.float32),
-            pltpu.SemaphoreType.DMA,
+            pltpu.SemaphoreType.DMA((tiles,)),
         ],
         {5 + len(accs): 0} if extra else None,
     )(state, pair, far, mask_x, part_sum, *accs, *extra)
@@ -410,23 +407,26 @@
         step *= 2
     count = half // step
     places = np.arange(span)
-    high = 2.0 * np.pi / span * ((np.arange(count)[:, None] * step * places[None]) % span)
+    period = max(2 * count, LANES)
+    high = 2.0 * np.pi / span * ((np.arange(count)[:, None] * step * places[None, :period]) % span)
     low = 2.0 * np.pi / span * ((np.arange(step)[:, None] * places[None]) % span)
-    tables = np.concatenate([np.cos(high), np.sin(high), np.cos(low), np.sin(low)])
-    return step, count, jnp.asarray(tables.astype(np.float32))
-
-
-def circulant_kernel(count, step, scale_ref, table_ref, high_ref, low_ref, band):
-    span = table_ref.shape[1]
+    tables = [np.concatenate([np.cos(a), np.sin(a)]) for a in (high, low)]
+    return step, count, [jnp.asarray(t.astype(np.float32)) for t in tables]
+
+
+def circulant_kernel(count, step, scale_ref, inner_ref, outer_ref, high_ref, low_ref, band):
+    period = inner_ref.shape[1]
+    span = outer_ref.shape[1]
     tall, wide = high_ref.shape
     dot = functools.partial(
         jnp.dot, precision=lax.Precision.HIGHEST, preferred_element_type=jnp.float32
     )
-    inner_cos = dot(scale_ref[...], table_ref[0:count])
-    inner_sin = dot(scale_ref[...], table_ref[count : 2 * count])
-    low_cos = table_ref[2 * count : 2 * count + step]
-    low_sin = table_ref[2 * count + step :]
-    line = jnp.sum(low_sin * inner_cos + low_cos * inner_sin, axis=0, keepdims=True)
+    repeat = span // period
+    inner_cos = jnp.concatenate([dot(scale_ref[...], inner_ref[:count])] * repeat, 1)
+    inner_sin = jnp.concatenate([dot(scale_ref[...], inner_ref[count:])] * repeat, 1)
+    line = jnp.sum(
+        outer_ref[step:] * inner_cos + outer_ref[:step] * inner_sin, axis=0, keepdims=True
+    )
     base = jnp.broadcast_to(-line, (ROWS, span))
     place = lax.broadcasted_iota(jnp.int32, (ROWS, span), 0)
     skew = base
@@ -460,11 +460,11 @@
         functools.partial(circulant_kernel, count, step),
         "circulant_band",
         1.0,
-        [PLACE, PLACE],
+        [PLACE, PLACE, PLACE],
         [PLACE, PLACE],
         [band, band],
         [pltpu.VMEM((tall, span), jnp.float32)],
-    )(scale, tables)
+    )(scale, *tables)
 
 
 def fill_lines(shards, x_refs):
@@ -568,46 +568,45 @@
         (i, i - 2) for i in range(3, slabs, 2)
     ]
     core = flip(state, 1)
-    bricks = pack_part(state, mask_x, BRICK_PARTS)
+    unit = rows_all // sum(BRICK_PARTS)
+    parts, start = [], 0
+    for share in BRICK_PARTS:
+        parts.append((start, share * unit))
+        start += share * unit
+    bricks = pack_part(state, mask_x, parts)
     pairs = [lax.ppermute(brick, "gx", swap) for brick in bricks]
     band = circulant(span_filter, span, width)
 
     masks = list(range(2, groups, 2))
     sums, lines = away_part(band, state, core, masks, SUM_PARTS, bricks[0])
     arrived = [
-        sum(
-            flip(sums[n * SUM_PARTS + c], mask) for n, mask in enumerate(masks)
-        )
+        sum(flip(sums[n * SUM_PARTS + c], mask) for n, mask in enumerate(masks))
         for c in range(SUM_PARTS)
     ]
     half = depth // 2
-    fars = []
+    wide = rows_all // SUM_PARTS
 
     def hand_on(c, after):
-        fars.append(lax.ppermute(pass_part(pairs[c], depth, after), "gx", carry))
-
-    hand_on(0, lines[0])
+        return lax.ppermute(pass_part(pairs[c], depth, after), "gx", carry)
+
     base = home_part(band, lines, state)
     acc_low = wall_part(state, mask_y, base, 0, half, lines[0])
-    hand_on(1, acc_low)
+    fars = [hand_on(0, acc_low)]
     acc_high = wall_part(state, mask_y, base, half, depth - half, acc_low)
-    for c in range(2, BRICK_PARTS):
-        hand_on(c, acc_high)
+    fars += [hand_on(c, acc_high) for c in range(1, len(parts))]
 
     out = None
-    step = rows_all // BRICK_PARTS
-    wide = rows_all // SUM_PARTS
-    for c in range(BRICK_PARTS):
+    for c, (start, _) in enumerate(parts):
         out = stream_part(
             state,
             pairs[c],
             fars[c],
             mask_x,
-            arrived[c * step // wide],
-            c * step % wide,
+            arrived[start // wide],
+            start % wide,
             [acc_low, acc_high],
             out,
-            c * step,
+            start,
         )
     return out
 

time: 55.9 us -> 52.8 us (0.945)
  starting transfers between devices: 22.5 us -> 18.7 us
  Pallas kernels: 24.9 us -> 22.9 us
  waiting for transfers between devices: 3.94 us -> 5.81 us
  local copies, waits for them, and re-layouts: 4.04 us -> 4.84 us
    ppermute x4 -> x3, starting transfers between devices: 14.8 us -> 11.7 us  [hand_on(): return lax.ppermute(pass_part(pairs[c], depth, after), 'gx', carry)]
    ppermute x4 -> x3, waiting for transfers between devices: 3.92 us -> 5.29 us  [per_device(): pairs = [lax.ppermute(brick, 'gx', swap) for brick in bricks]]
    pallas_call x4 -> x3, Pallas kernels: 10.8 us -> 9.46 us  [stream_part(): call(functools.partial(stream_kernel, start, sum_start, counts), 'stream_...]
    squeeze x0 -> x1, local copies, waits for them, and re-layouts: none -> 0.84 us  [pack_part(): mask_x[0]]
    ppermute x4 -> x3, starting transfers between devices: 4.66 us -> 4.53 us  [per_device(): pairs = [lax.ppermute(brick, 'gx', swap) for brick in bricks]]
    unnamed x14 -> x22, local copies, waits for them, and re-layouts: 3.9 us -> 3.85 us
  transfers between devices with their start and end apart: 11 -> 9, of which waited for: 2 -> 4; matrix products, arithmetic and copies ran while one was open for 0% -> 2% of each run, Pallas kernels for 40% -> 39%
where the time goes in v1:
time: 52.8 us; the launch traced here: 52.5 us
  Pallas kernels  22.9 us (43%)
  starting transfers between devices  18.7 us (35%)
  waiting for transfers between devices  5.81 us (11%)
  local copies, waits for them, and re-layouts  4.84 us (9%)
    ppermute x3, starting transfers between devices, hand_on(): return lax.ppermute(pass_part(pairs[c], depth, after), 'gx', carry)  11.7 us
    pallas_call x3, Pallas kernels, stream_part(): call(functools.partial(stream_kernel, start, sum_start, counts), 'stream_...  9.46 us
    pallas_call x2, Pallas kernels, wall_part(): call(kernel, 'wall_faces', 5.0 * count / depth, [PLACE, PLACE, PLACE, ANY...  5.9 us
    ppermute x3, waiting for transfers between devices, per_device(): pairs = [lax.ppermute(brick, 'gx', swap) for brick in bricks]  5.29 us
    ppermute x3, starting transfers between devices, per_device(): pairs = [lax.ppermute(brick, 'gx', swap) for brick in bricks]  4.53 us
    unnamed x22, local copies, waits for them, and re-layouts  3.85 us
    pallas_call x1, Pallas kernels, away_part(): call(functools.partial(away_kernel, masks, parts), 'span_away', 3.0, [PLA...  3.52 us
    ppermute x3, starting transfers between devices, flip(): return lax.ppermute(array, 'gz', [(g, g ^ bit) for g in range(groups)])  2.54 us
  transfers between devices with their start and end apart: 9, of which 4 were waited for; matrix products, arithmetic and copies ran while one was open for 2% of the time, Pallas kernels for 39%

profile of v1, /device:TPU:0, one launch (start us, length us, event | category | flops | bytes accessed | tf_op | source)
XLA Modules:
  0.0 52.5 jit_solution(7480504349552592848)
XLA Ops:
  0.0 0.0 copy-start.5
  0.0 0.0 copy-start.10
  0.0 0.5 collective-permute-start.1
  0.5 0.8 %slice_bitcast_fusion.mask_ref = s32[32,512]{1,0:T(8,128)S(1)} fusion(s32[4,32,512]{2,1,0:T(8,128)} %refs_3_.5), kind=kLoop, calls=%fused_computation | loop fusion | bytes 131072 | tf_op jit(solution)/shard_map/squeeze | solution.py:231
  1.3 0.0 copy-start
  1.3 1.3 %copy-done = f32[5,4,32,512]{3,2,1,0:T(8,128)S(1)} copy-done((f32[5,4,32,512]{3,2,1,0:T(8,128)S(1)}, f32[5,4,32,512]{3,2,1,0:T(8,128)}, u32[]{:S(2)}) %copy-start) | copy-done | bytes 1310744
  2.6 0.0 copy-start.1
  2.6 1.0 %pack_bricks.1 = (f32[21,16,512]{2,1,0:T(8,128)}, f32[21,8,512]{2,1,0:T(8,128)S(1)}, f32[21,8,512]{2,1,0:T(8,128)S(1)}) custom-call(f32[20,32,512]{2,1,0:T(8,128)S(1)} %bitcast.4, s32[32,512]{1,0:T(8,128)S(1)} %slice_bitcast_fusion.mask_ref), custom_call_target="tpu_custom_call" | custom-call | flops 50000000 | bytes 150000 | tf_op jit(solution)/shard_map/pack_bricks/pallas_call | solution.py:224
  3.7 0.7 %copy-done.6 = f32[21,8,512]{2,1,0:T(8,128)} copy-done((f32[21,8,512]{2,1,0:T(8,128)}, f32[21,8,512]{2,1,0:T(8,128)S(1)}, u32[]{:S(2)}) %copy-start.6) | copy-done | bytes 344088
  4.4 0.7 %copy-done.8 = f32[21,8,512]{2,1,0:T(8,128)} copy-done((f32[21,8,512]{2,1,0:T(8,128)}, f32[21,8,512]{2,1,0:T(8,128)S(1)}, u32[]{:S(2)}) %copy-start.8) | copy-done | bytes 344088
  5.1 2.5 %collective-permute-start.6 = (f32[21,16,512]{2,1,0:T(8,128)}, f32[21,16,512]{2,1,0:T(8,128)S(1)}, u32[]{:S(2)}, u32[]{:S(2)}) collective-permute-start(f32[21,16,512]{2,1,0:T(8,128)} %get-tuple-element.17.after_ref), channel_id=1, source_target_pairs={{0,4},{4,0},{8,12},{12,8},{16,20},{20,16},{24,28},{28,24},{1,5},{5... | collective-permute-start | bytes 2064392 | tf_op jit(solution)/shard_map/ppermute | solution.py:577
  7.6 0.0 copy-done.10
  7.6 0.1 reshape.7
  7.7 0.1 copy.9
  7.8 0.0 copy-done.5
  7.8 1.0 %copy-done.4 = f32[64,2048]{1,0:T(8,128)S(1)} copy-done((f32[64,2048]{1,0:T(8,128)S(1)}, f32[64,2048]{1,0:T(8,128)}, u32[]{:S(2)}) %copy-start.4) | copy-done | bytes 524312
  8.8 0.7 %circulant_band.1 = (bf16[256,2560]{1,0:T(8,128)(2,1)S(1)}, bf16[256,2560]{1,0:T(8,128)(2,1)S(1)}) custom-call(f32[32,32]{1,0:T(8,128)S(1)} %bitcast.5, f32[64,128]{1,0:T(8,128)S(1)} %copy-done.5, f32[64,2048]{1,0:T(8,128)S(1)} %copy-done.4), custom_call_target="tpu_custom_call" | custom-call | flops 100000000 | bytes 300000 | tf_op jit(solution)/shard_map/circulant_band/pallas_call | solution.py:459
  9.6 0.0 collective-permute-done.1.core_ref
  9.6 0.0 copy-done.1
  9.6 0.0 copy-start.9
  9.6 0.0 copy-start.7
  9.6 3.5 %span_away.1 = (f32[5,4,16,512]{3,2,1,0:T(8,128)S(1)}, f32[5,4,16,512]{3,2,1,0:T(8,128)S(1)}, bf16[640,1024]{1,0:T(8,128)(2,1)S(1)}, bf16[640,1024]{1,0:T(8,128)(2,1)S(1)}) custom-call(bf16[256,2560]{1,0:T(8,128)(2,1)S(1)} %get-tuple-element.15.high_ref, bf16[256,2560]{1,0:T(8,128)(2,1)S(1)} %get-tuple-element.16.low_ref, f32[5,4,32,512]{3,2,1,0:T(8,128)S(1)} %copy-done.1, ...), custom_call_target="tpu_custom_call" | custom-call | flops 300000000 | bytes 900000 | tf_op jit(solution)/shard_map/span_away/pallas_call | solution.py:526
  13.1 1.6 %collective-permute-start.8 = (f32[5,4,16,512]{3,2,1,0:T(8,128)S(1)}, f32[5,4,16,512]{3,2,1,0:T(8,128)S(1)}, u32[]{:S(2)}, u32[]{:S(2)}) collective-permute-start(f32[5,4,16,512]{3,2,1,0:T(8,128)S(1)} %get-tuple-element.22), channel_id=1, source_target_pairs={{0,2},{1,3},{2,0},{3,1},{4,6},{5,7},{6,4},{7,5},{8,10},{9,11},{10,... | collective-permute-start | bytes 1966088 | tf_op jit(solution)/shard_map/ppermute | solution.py:564
  14.7 0.5 collective-permute-start.3
  15.2 0.0 copy-done.9
  15.2 0.1 collective-permute-start.4
  15.3 0.0 copy-done.7
  15.3 1.9 %collective-permute-start = (f32[21,8,512]{2,1,0:T(8,128)S(1)}, f32[21,8,512]{2,1,0:T(8,128)S(1)}, u32[]{:S(2)}, u32[]{:S(2)}) collective-permute-start(f32[21,8,512]{2,1,0:T(8,128)S(1)} %copy-done.7), channel_id=1, source_target_pairs={{0,4},{4,0},{8,12},{12,8},{16,20},{20,16},{24,28},{28,24},{1,5},{5... | collective-permute-start | bytes 1032200 | tf_op jit(solution)/shard_map/ppermute | solution.py:577
  17.3 2.2 %span_home.1.base_ref = f32[5,4,32,512]{3,2,1,0:T(8,128)S(1)} custom-call(bf16[256,2560]{1,0:T(8,128)(2,1)S(1)} %get-tuple-element.15.high_ref, bf16[256,2560]{1,0:T(8,128)(2,1)S(1)} %get-tuple-element.16.low_ref, bf16[640,1024]{1,0:T(8,128)(2,1)S(1)} %get-tuple-element.18.xh.after_ref, bf16[640,1024]{1,0:T(8,128)(2,1)S(1)} %get-tuple-element.19.xl, ...), custom_call_target="tpu_custom_call" | custom-call | flops 200000000 | bytes 600000 | tf_op jit(solution)/shard_map/span_home/pallas_call | solution.py:546
  19.5 0.0 copy-done.3
  19.5 3.0 %wall_faces.2.after_ref.refs_5_ = f32[5,2,32,512]{3,2,1,0:T(8,128)S(1)} custom-call(f32[5,4,32,512]{3,2,1,0:T(8,128)S(1)} %copy-done.1, s32[4,32,512]{2,1,0:T(8,128)S(1)} %copy-done.3, f32[5,4,32,512]{3,2,1,0:T(8,128)S(1)} %span_home.1.base_ref, bf16[640,1024]{1,0:T(8,128)(2,1)S(1)} %get-tuple-element.18.xh.after_ref), custom_call_target="tpu_custom_call" | custom-call | flops 250000000 | bytes 750000 | tf_op jit(solution)/shard_map/wall_faces/pallas_call | solution.py:198
  22.4 1.7 %collective-permute-done.6.pair_ref.refs_1_ = f32[21,16,512]{2,1,0:T(8,128)S(1)} collective-permute-done((f32[21,16,512]{2,1,0:T(8,128)}, f32[21,16,512]{2,1,0:T(8,128)S(1)}, u32[]{:S(2)}, u32[]{:S(2)}) %collective-permute-start.6) | collective-permute-done | bytes 688160 | tf_op jit(solution)/shard_map/ppermute | solution.py:577
  24.2 4.0 %collective-permute-start.7 = (f32[16,16,512]{2,1,0:T(8,128)S(1)}, f32[16,16,512]{2,1,0:T(8,128)S(1)}, u32[]{:S(2)}, u32[]{:S(2)}) collective-permute-start(f32[16,16,512]{2,1,0:T(8,128)S(1)} %pass_planes.5), channel_id=1, source_target_pairs={{0,8},{8,16},{16,24},{12,4},{20,12},{28,20},{1,9},{9,17},{17,25},{... | collective-permute-start | bytes 1572872 | tf_op jit(solution)/shard_map/ppermute | solution.py:590
  28.1 3.0 %wall_faces.3.after_ref.refs_6_ = f32[5,2,32,512]{3,2,1,0:T(8,128)S(1)} custom-call(f32[5,4,32,512]{3,2,1,0:T(8,128)S(1)} %copy-done.1, s32[4,32,512]{2,1,0:T(8,128)S(1)} %copy-done.3, f32[5,4,32,512]{3,2,1,0:T(8,128)S(1)} %span_home.1.base_ref, f32[5,2,32,512]{3,2,1,0:T(8,128)S(1)} %wall_faces.2.after_ref.refs_5_), custom_call_target="tpu_custom_call" | custom-call | flops 250000000 | bytes 750000 | tf_op jit(solution)/shard_map/wall_faces/pallas_call | solution.py:198
  31.1 0.0 copy-start.2
  31.1 0.4 collective-permute-done.4.pair_ref.refs_1_
  31.5 4.0 %collective-permute-start.5 = (f32[16,8,512]{2,1,0:T(8,128)S(1)}, f32[16,8,512]{2,1,0:T(8,128)S(1)}, u32[]{:S(2)}, u32[]{:S(2)}) collective-permute-start(f32[16,8,512]{2,1,0:T(8,128)S(1)} %pass_planes.4), channel_id=1, source_target_pairs={{0,8},{8,16},{16,24},{12,4},{20,12},{28,20},{1,9},{9,17},{17,25},{... | collective-permute-start | bytes 786440 | tf_op jit(solution)/shard_map/ppermute | solution.py:590
  35.5 3.2 %collective-permute-done.pair_ref.refs_1_ = f32[21,8,512]{2,1,0:T(8,128)S(1)} collective-permute-done((f32[21,8,512]{2,1,0:T(8,128)S(1)}, f32[21,8,512]{2,1,0:T(8,128)S(1)}, u32[]{:S(2)}, u32[]{:S(2)}) %collective-permute-start) | collective-permute-done | bytes 344096 | tf_op jit(solution)/shard_map/ppermute | solution.py:577
  38.7 3.7 %collective-permute-start.2 = (f32[16,8,512]{2,1,0:T(8,128)S(1)}, f32[16,8,512]{2,1,0:T(8,128)S(1)}, u32[]{:S(2)}, u32[]{:S(2)}) collective-permute-start(f32[16,8,512]{2,1,0:T(8,128)S(1)} %pass_planes.3), channel_id=1, source_target_pairs={{0,8},{8,16},{16,24},{12,4},{20,12},{28,20},{1,9},{9,17},{17,25},{... | collective-permute-start | bytes 786440 | tf_op jit(solution)/shard_map/ppermute | solution.py:590
  42.5 0.0 collective-permute-done.7.refs_2_
  42.5 0.0 collective-permute-done.8.refs_4_
  42.5 0.0 copy-done.2
  42.5 4.4 %stream_faces.3.refs_7_ = f32[5,4,32,512]{3,2,1,0:T(8,128)} custom-call(f32[5,4,32,512]{3,2,1,0:T(8,128)S(1)} %copy-done.1, f32[21,16,512]{2,1,0:T(8,128)S(1)} %collective-permute-done.6.pair_ref.refs_1_, f32[16,16,512]{2,1,0:T(8,128)S(1)} %collective-permute-done.7.refs_2_, s32[4,32,512]{2,1,0:T(8,128)S(1)} %copy-done.2, ...), custom_call_target="tpu_custom_call" | custom-call | flops 400000000 | bytes 1200000 | tf_op jit(solution)/shard_map/stream_faces/pallas_call | solution.py:384
  46.9 0.0 collective-permute-done.5.refs_2_
  46.9 0.0 collective-permute-done.3.refs_4_
  46.9 2.5 %stream_faces.4.refs_7_ = f32[5,4,32,512]{3,2,1,0:T(8,128)} custom-call(f32[5,4,32,512]{3,2,1,0:T(8,128)S(1)} %copy-done.1, f32[21,8,512]{2,1,0:T(8,128)S(1)} %collective-permute-done.4.pair_ref.refs_1_, f32[16,8,512]{2,1,0:T(8,128)S(1)} %collective-permute-done.5.refs_2_, s32[4,32,512]{2,1,0:T(8,128)S(1)} %copy-done.2, ...), custom_call_target="tpu_custom_call", output_to_operand_aliasing={{}: (7, {})} | custom-call | flops 200000000 | bytes 600000 | tf_op jit(solution)/shard_map/stream_faces/pallas_call | solution.py:384
  49.5 0.5 collective-permute-done.2.refs_2_
  50.0 2.5 %stream_faces.5 = f32[5,4,32,512]{3,2,1,0:T(8,128)} custom-call(f32[5,4,32,512]{3,2,1,0:T(8,128)S(1)} %copy-done.1, f32[21,8,512]{2,1,0:T(8,128)S(1)} %collective-permute-done.pair_ref.refs_1_, f32[16,8,512]{2,1,0:T(8,128)S(1)} %collective-permute-done.2.refs_2_, s32[4,32,512]{2,1,0:T(8,128)S(1)} %copy-done.2, ...), custom_call_target="tpu_custom_call", output_to_operand_aliasing={{}: (7, {})} | custom-call | flops 200000000 | bytes 600000 | tf_op jit(solution)/shard_map/stream_faces/pallas_call | solution.py:384
  (8 shorter events, 0.1 us)
Async XLA Ops:
  0.0 7.8 %copy-start.5 = (f32[64,128]{1,0:T(8,128)S(1)}, f32[64,128]{1,0:T(8,128)}, u32[]{:S(2)}) copy-start(f32[64,128]{1,0:T(8,128)} %constant.6.clone.inner_ref) | copy-start | bytes 98308
  0.0 7.6 %copy-start.10 = (f32[1024]{0:T(1024)S(1)}, f32[1024]{0:T(1024)}, u32[]{:S(2)}) copy-start(f32[1024]{0:T(1024)} %param.9) | copy-start | bytes 12292
  0.0 9.6 %collective-permute-start.1 = (f32[5,4,32,512]{3,2,1,0:T(8,128)}, f32[5,4,32,512]{3,2,1,0:T(8,128)S(1)}, u32[]{:S(2)}, u32[]{:S(2)}) collective-permute-start(f32[5,4,32,512]{3,2,1,0:T(8,128)} %refs_0_.5), channel_id=1, source_target_pairs={{0,1},{1,0},{2,3},{3,2},{4,5},{5,4},{6,7},{7,6},{8,9},{9,8},{10,11... | collective-permute-start | bytes 3932168 | tf_op jit(solution)/shard_map/ppermute | solution.py:564
  1.3 1.3 %copy-start = (f32[5,4,32,512]{3,2,1,0:T(8,128)S(1)}, f32[5,4,32,512]{3,2,1,0:T(8,128)}, u32[]{:S(2)}) copy-start(f32[5,4,32,512]{3,2,1,0:T(8,128)} %refs_0_.5) | copy-start | bytes 3932164
  2.6 7.0 %copy-start.1 = (f32[5,4,32,512]{3,2,1,0:T(8,128)S(1)}, f32[5,4,32,512]{3,2,1,0:T(8,128)}, u32[]{:S(2)}) copy-start(f32[5,4,32,512]{3,2,1,0:T(8,128)} %refs_0_.5) | copy-start | bytes 3932164
  3.7 0.7 %copy-start.6 = (f32[21,8,512]{2,1,0:T(8,128)}, f32[21,8,512]{2,1,0:T(8,128)S(1)}, u32[]{:S(2)}) copy-start(f32[21,8,512]{2,1,0:T(8,128)S(1)} %get-tuple-element.14) | copy-start | bytes 1032196
  4.4 0.7 %copy-start.8 = (f32[21,8,512]{2,1,0:T(8,128)}, f32[21,8,512]{2,1,0:T(8,128)S(1)}, u32[]{:S(2)}) copy-start(f32[21,8,512]{2,1,0:T(8,128)S(1)} %get-tuple-element.21) | copy-start | bytes 1032196
  5.1 19.0 %collective-permute-start.6 = (f32[21,16,512]{2,1,0:T(8,128)}, f32[21,16,512]{2,1,0:T(8,128)S(1)}, u32[]{:S(2)}, u32[]{:S(2)}) collective-permute-start(f32[21,16,512]{2,1,0:T(8,128)} %get-tuple-element.17.after_ref), channel_id=1, source_target_pairs={{0,4},{4,0},{8,12},{12,8},{16,20},{20,16},{24,28},{28,24},{1,5},{5... | collective-permute-start | bytes 2064392 | tf_op jit(solution)/shard_map/ppermute | solution.py:577
  7.8 1.0 %copy-start.4 = (f32[64,2048]{1,0:T(8,128)S(1)}, f32[64,2048]{1,0:T(8,128)}, u32[]{:S(2)}) copy-start(f32[64,2048]{1,0:T(8,128)} %constant.7.clone.outer_ref) | copy-start | bytes 1572868
  9.6 5.6 %copy-start.9 = (f32[21,8,512]{2,1,0:T(8,128)S(1)}, f32[21,8,512]{2,1,0:T(8,128)}, u32[]{:S(2)}) copy-start(f32[21,8,512]{2,1,0:T(8,128)} %copy-done.8) | copy-start | bytes 1032196
  9.6 5.7 %copy-start.7 = (f32[21,8,512]{2,1,0:T(8,128)S(1)}, f32[21,8,512]{2,1,0:T(8,128)}, u32[]{:S(2)}) copy-start(f32[21,8,512]{2,1,0:T(8,128)} %copy-done.6) | copy-start | bytes 1032196
  13.1 29.3 %collective-permute-start.8 = (f32[5,4,16,512]{3,2,1,0:T(8,128)S(1)}, f32[5,4,16,512]{3,2,1,0:T(8,128)S(1)}, u32[]{:S(2)}, u32[]{:S(2)}) collective-permute-start(f32[5,4,16,512]{3,2,1,0:T(8,128)S(1)} %get-tuple-element.22), channel_id=1, source_target_pairs={{0,2},{1,3},{2,0},{3,1},{4,6},{5,7},{6,4},{7,5},{8,10},{9,11},{10,... | collective-permute-start | bytes 1966088 | tf_op jit(solution)/shard_map/ppermute | solution.py:564
  14.7 32.2 %collective-permute-start.3 = (f32[5,4,16,512]{3,2,1,0:T(8,128)S(1)}, f32[5,4,16,512]{3,2,1,0:T(8,128)S(1)}, u32[]{:S(2)}, u32[]{:S(2)}) collective-permute-start(f32[5,4,16,512]{3,2,1,0:T(8,128)S(1)} %get-tuple-element.20), channel_id=1, source_target_pairs={{0,2},{1,3},{2,0},{3,1},{4,6},{5,7},{6,4},{7,5},{8,10},{9,11},{10,... | collective-permute-start | bytes 1966088 | tf_op jit(solution)/shard_map/ppermute | solution.py:564
  15.2 16.3 %collective-permute-start.4 = (f32[21,8,512]{2,1,0:T(8,128)S(1)}, f32[21,8,512]{2,1,0:T(8,128)S(1)}, u32[]{:S(2)}, u32[]{:S(2)}) collective-permute-start(f32[21,8,512]{2,1,0:T(8,128)S(1)} %copy-done.9), channel_id=1, source_target_pairs={{0,4},{4,0},{8,12},{12,8},{16,20},{20,16},{24,28},{28,24},{1,5},{5... | collective-permute-start | bytes 1032200 | tf_op jit(solution)/shard_map/ppermute | solution.py:577
  15.3 23.3 %collective-permute-start = (f32[21,8,512]{2,1,0:T(8,128)S(1)}, f32[21,8,512]{2,1,0:T(8,128)S(1)}, u32[]{:S(2)}, u32[]{:S(2)}) collective-permute-start(f32[21,8,512]{2,1,0:T(8,128)S(1)} %copy-done.7), channel_id=1, source_target_pairs={{0,4},{4,0},{8,12},{12,8},{16,20},{20,16},{24,28},{28,24},{1,5},{5... | collective-permute-start | bytes 1032200 | tf_op jit(solution)/shard_map/ppermute | solution.py:577
  17.3 2.2 %copy-start.3 = (s32[4,32,512]{2,1,0:T(8,128)S(1)}, s32[4,32,512]{2,1,0:T(8,128)}, u32[]{:S(2)}) copy-start(s32[4,32,512]{2,1,0:T(8,128)} %mask_ref.3) | copy-start | bytes 786436
  24.2 18.3 %collective-permute-start.7 = (f32[16,16,512]{2,1,0:T(8,128)S(1)}, f32[16,16,512]{2,1,0:T(8,128)S(1)}, u32[]{:S(2)}, u32[]{:S(2)}) collective-permute-start(f32[16,16,512]{2,1,0:T(8,128)S(1)} %pass_planes.5), channel_id=1, source_target_pairs={{0,8},{8,16},{16,24},{12,4},{20,12},{28,20},{1,9},{9,17},{17,25},{... | collective-permute-start | bytes 1572872 | tf_op jit(solution)/shard_map/ppermute | solution.py:590
  31.1 11.4 %copy-start.2 = (s32[4,32,512]{2,1,0:T(8,128)S(1)}, s32[4,32,512]{2,1,0:T(8,128)}, u32[]{:S(2)}) copy-start(s32[4,32,512]{2,1,0:T(8,128)} %refs_3_.5) | copy-start | bytes 786436
  31.5 15.4 %collective-permute-start.5 = (f32[16,8,512]{2,1,0:T(8,128)S(1)}, f32[16,8,512]{2,1,0:T(8,128)S(1)}, u32[]{:S(2)}, u32[]{:S(2)}) collective-permute-start(f32[16,8,512]{2,1,0:T(8,128)S(1)} %pass_planes.4), channel_id=1, source_target_pairs={{0,8},{8,16},{16,24},{12,4},{20,12},{28,20},{1,9},{9,17},{17,25},{... | collective-permute-start | bytes 786440 | tf_op jit(solution)/shard_map/ppermute | solution.py:590
  38.7 11.3 %collective-permute-start.2 = (f32[16,8,512]{2,1,0:T(8,128)S(1)}, f32[16,8,512]{2,1,0:T(8,128)S(1)}, u32[]{:S(2)}, u32[]{:S(2)}) collective-permute-start(f32[16,8,512]{2,1,0:T(8,128)S(1)} %pass_planes.3), channel_id=1, source_target_pairs={{0,8},{8,16},{16,24},{12,4},{20,12},{28,20},{1,9},{9,17},{17,25},{... | collective-permute-start | bytes 786440 | tf_op jit(solution)/shard_map/ppermute | solution.py:590
